TPU v7x, 512 devices: a whole 4x8x8 slice. The times are simulated.
512 devices in a mesh: dp: 16 (over y, core), mp: 32 (over x, z).
Axes of the slice: x: 4, y: 8, z: 8, core: 2. Of those that a mesh axis runs over, the one named last changes fastest.
Arguments:
- packed_rows: bfloat16 [16384, 6144], P(('dp', 'mp')), may hold values from -6 to 6
- dest_group: int32 [16384], P(('dp', 'mp')), may hold values from 0 to 15, as said below
- dest_slot: int32 [16384], P(('dp', 'mp')), may hold values from 0 to 31, as said below
- image_ids: int32 [16, 1024], P('dp', 'mp'), may hold values from 0 to 15, never falling along the last dimension, each value on 1 to 512 neighbouring positions
- ln_gain: float32 [6144], replicated, may hold values from 0.1 to 1.9
- qkv_weight: bfloat16 [3, 6144, 4096], P(None, None, 'mp'), may hold values from -0.078125 to 0.078125
- qk_gain: float32 [2, 4096], P(None, 'mp'), may hold values from 0.6 to 8
Outputs:
- attended: bfloat16 [16384, 4096], P(('dp', 'mp'))
Inputs may be any that keep to these rules, and one draw needn't show every extreme that they name: `dest_group`: rows of the loader at mp index m go to tokens m * 32 to (m + 1) * 32 - 1 of their group. Each loader device sends at most 4 rows to one group, and in every draw some loader device sends exactly 4 rows to one group. `dest_slot`: together with dest_group, every slot of every receiving device gets exactly one row.
All inputs are finite; a program needn't handle non-finite values.
Results may differ from a plain program's by a relative error of at most 0.022.
The roundings to bfloat16 on the way count: a program that leaves them out, or rounds other values in their place, can miss the bound.
Values may be sent and summed in bfloat16 or wider, within the bound.
No kernel may reach another device: no remote copies, remote signals or barrier semaphores. Data moves between devices by JAX's collectives and lax.ppermute only.
A program may use at most 64 MiB of HBM per device.

v0:
```python
import jax
import jax.numpy as jnp
from jax import lax
from jax.sharding import PartitionSpec as P

HD = 128


def norm_rows(rows, gain):
    values = rows.astype(jnp.float32)
    mean = jnp.mean(values, axis=-1, keepdims=True)
    centered = values - mean
    spread = jnp.mean(centered * centered, axis=-1, keepdims=True)
    return (centered * lax.rsqrt(spread + 1e-06) * gain).astype(jnp.bfloat16)


def local(packed_rows, dest_group, dest_slot, image_ids, ln_gain, qkv_weight, qk_gain):
    normed = norm_rows(packed_rows, ln_gain)
    tok_rows = packed_rows.shape[0]
    width = packed_rows.shape[1]
    n_groups = lax.axis_size("dp")
    capacity = max(2, 2 * tok_rows // n_groups)
    positions = jnp.arange(tok_rows, dtype=jnp.int32)
    earlier = (dest_group[:, None] == dest_group[None, :]) & (
        positions[None, :] < positions[:, None]
    )
    rank = jnp.sum(earlier.astype(jnp.int32), axis=1)
    send_rows = (
        jnp.zeros((n_groups, capacity, width), jnp.bfloat16).at[dest_group, rank].set(normed)
    )
    send_slots = (
        jnp.full((n_groups, capacity), -1.0, jnp.bfloat16)
        .at[dest_group, rank]
        .set(dest_slot.astype(jnp.bfloat16))
    )
    got_rows, got_slots = (
        lax.all_to_all(send_rows, "dp", split_axis=0, concat_axis=0, tiled=True),
        lax.all_to_all(send_slots, "dp", split_axis=0, concat_axis=0, tiled=True),
    )
    flat_rows = got_rows.reshape(n_groups * capacity, width)
    flat_slots = got_slots.reshape(n_groups * capacity).astype(jnp.float32)
    placing = (flat_slots[None, :] == positions[:, None].astype(jnp.float32)).astype(jnp.bfloat16)
    tokens = jnp.dot(placing, flat_rows, preferred_element_type=jnp.float32).astype(jnp.bfloat16)
    group_rows, group_ids = (
        lax.all_gather(tokens, "mp", axis=0, tiled=True),
        lax.all_gather(image_ids[0].astype(jnp.bfloat16), "mp", axis=0, tiled=True),
    )
    count = group_rows.shape[0]
    heads = qkv_weight.shape[2] // HD
    projected = jnp.einsum(
        "td,kdc->ktc", group_rows, qkv_weight, preferred_element_type=jnp.float32
    )
    query_n = norm_rows(projected[0].reshape(count, heads, HD), qk_gain[0].reshape(heads, HD))
    key_n = norm_rows(projected[1].reshape(count, heads, HD), qk_gain[1].reshape(heads, HD))
    value = projected[2].astype(jnp.bfloat16).reshape(count, heads, HD)
    scores = jnp.einsum(
        "qhc,khc->hqk", query_n, key_n, preferred_element_type=jnp.float32
    ) * HD ** (-0.5)
    image_f = group_ids.astype(jnp.float32)
    same = image_f[:, None] == image_f[None, :]
    masked = jnp.where(same[None], scores, -1e30)
    top = jnp.max(masked, axis=-1, keepdims=True)
    weights = jnp.exp(masked - top)
    probs = (weights / jnp.sum(weights, axis=-1, keepdims=True)).astype(jnp.bfloat16)
    result = jnp.einsum("hqk,khc->qhc", probs, value, preferred_element_type=jnp.float32)
    result = result.astype(jnp.bfloat16).reshape(count, heads * HD)
    return lax.all_to_all(result, "mp", split_axis=0, concat_axis=1, tiled=True)


def solution(mesh):
    return jax.shard_map(
        local,
        mesh=mesh,
        in_specs=(
            P(("dp", "mp"), None),
            P(("dp", "mp")),
            P(("dp", "mp")),
            P("dp", "mp"),
            P(),
            P(None, None, "mp"),
            P(None, "mp"),
        ),
        out_specs=P(("dp", "mp"), None),
        check_vma=False,
    )
```

profile of v0, /device:TPU:8, one launch (start us, length us, event | category | flops | bytes accessed | tf_op | source)
XLA Modules:
  0.0 229.7 jit_solution(2317695493599553311)
XLA Ops:
  6.5 0.9 convert_reduce_fusion.1
  7.4 0.7 fusion.39
  8.1 0.7 convert_element_type.105
  8.8 2.1 scatter_fusion
  10.8 0.7 copy.22
  11.5 9.1 %all-to-all-start = ((bf16[16,1,4]{2,1,0:T(2,128)(2,1)}), bf16[16,1,4]{2,1,0:T(2,128)(2,1)S(1)}, u32[]{:S(2)}, u32[]{:S(2)}) async-start(bf16[16,1,4]{2,1,0:T(2,128)(2,1)} %copy.22), calls=%async_computation | async-start | bytes 16384 | tf_op jit(solution)/shard_map/all_to_all | solution.py:38
  20.6 1.2 convert_reduce_fusion
  21.8 1.3 fusion.7
  23.1 1.2 fusion.9
  24.3 1.2 broadcast_in_dim.11
  25.5 10.3 %scatter_fusion.1 = bf16[16,4,6144]{2,1,0:T(4,128)(2,1)} fusion(bf16[16,4,6144]{2,1,0:T(4,128)(2,1)} %broadcast_in_dim.11, s32[32]{0:T(128)S(1)} %fusion.39, bf16[32,6144]{1,0:T(8,128)(2,1)S(1)} %fusion.9), kind=kCustom, calls=%fused_computation.1 | custom fusion | bytes 1179904 | tf_op jit(solution)/shard_map/scatter | solution.py:29
  35.7 7.2 %all-to-all-start.1 = ((bf16[16,4,6144]{2,1,0:T(4,128)(2,1)}), bf16[16,4,6144]{2,1,0:T(4,128)(2,1)S(1)}, u32[]{:S(2)}, u32[]{:S(2)}) async-start(bf16[16,4,6144]{2,1,0:T(4,128)(2,1)} %scatter_fusion.1), calls=%async_computation.1 | async-start | bytes 1572864 | tf_op jit(solution)/shard_map/all_to_all | solution.py:37
  43.1 18.9 %all-to-all-done.1 = bf16[16,4,6144]{2,1,0:T(4,128)(2,1)S(1)} async-done(((bf16[16,4,6144]{2,1,0:T(4,128)(2,1)}), bf16[16,4,6144]{2,1,0:T(4,128)(2,1)S(1)}, u32[]{:S(2)}, u32[]{:S(2)}) %all-to-all-start.1) | async-done | bytes 786464 | tf_op jit(solution)/shard_map/all_to_all | solution.py:37
  62.2 1.1 convolution_convert_fusion
  63.4 6.6 %copy.23 = bf16[3,6144,128]{1,2,0:T(8,128)(2,1)} copy(bf16[3,6144,128]{2,1,0:T(8,128)(2,1)} %param.12) | data formatting | bytes 9437184 | tf_op args[5]
  70.0 1.3 dynamic-slice
  72.2 80.0 %all-reduce = bf16[1024]{0:T(1024)(128)(2,1)S(1)} all-reduce(bf16[1024]{0:T(1024)(128)(2,1)S(1)} %dynamic-update-slice), channel_id=2, replica_groups=mesh['dp'=16,'mp'=32] {'mp'}, use_global_device_ids=true, to_apply=%add | all-reduce | flops 1024 | bytes 4096
  152.3 39.4 %all-gather.3.cloned.1.call-done = bf16[1024,6144]{1,0:T(8,128)(2,1)} async-done(((bf16[32,6144]{1,0:T(8,128)(2,1)}), bf16[1024,6144]{1,0:T(8,128)(2,1)}) %all-gather.3.cloned.1.call-update) | async-done | bytes 12582928 | tf_op jit(solution)/shard_map/all_gather | solution.py:45
  191.7 9.4 %fusion.42 = f32[1024,384]{0,1:S(1)} fusion(bf16[1024,6144]{1,0:T(8,128)(2,1)} %all-gather.3.cloned.1.call-done, bf16[6144,384]{0,1:T(8,128)(2,1)} %bitcast.92), kind=kOutput, calls=%fused_computation.73 | convolution fusion | flops 4831838208 | bytes 18874368
  201.4 1.0 fusion.1
  202.3 1.0 fusion
  203.4 1.4 fusion.4
  204.9 17.2 %all_to_all.33 = bf16[32,32,128]{2,1,0:T(8,128)(2,1)S(1)} all-to-all(bf16[32,32,128]{2,1,0:T(8,128)(2,1)S(1)} %bitcast.97), channel_id=1, replica_groups=mesh['dp'=16,'mp'=32] {'mp'}, dimensions={0} | all-to-all | bytes 524288 | tf_op jit(solution)/shard_map/all_to_all | solution.py:67
  222.1 0.7 copy_bitcast_fusion
  (25 shorter events, 1.0 us)
Async XLA Ops:
  11.5 24.2 %all-to-all-start = ((bf16[16,1,4]{2,1,0:T(2,128)(2,1)}), bf16[16,1,4]{2,1,0:T(2,128)(2,1)S(1)}, u32[]{:S(2)}, u32[]{:S(2)}) async-start(bf16[16,1,4]{2,1,0:T(2,128)(2,1)} %copy.22), calls=%async_computation | async-start | bytes 16384 | tf_op jit(solution)/shard_map/all_to_all | solution.py:38
  35.7 26.3 %all-to-all-start.1 = ((bf16[16,4,6144]{2,1,0:T(4,128)(2,1)}), bf16[16,4,6144]{2,1,0:T(4,128)(2,1)S(1)}, u32[]{:S(2)}, u32[]{:S(2)}) async-start(bf16[16,4,6144]{2,1,0:T(4,128)(2,1)} %scatter_fusion.1), calls=%async_computation.1 | async-start | bytes 1572864 | tf_op jit(solution)/shard_map/all_to_all | solution.py:37
  43.0 148.7 %all-gather.3.cloned.1.call-start = ((), (), s32[]{:S(2)}) async-start(), calls=%async_computation.3 | async-start | bytes 12976128 | tf_op jit(solution)/shard_map/all_gather | solution.py:45
  63.4 8.6 %copy-start.1 = (s32[1,32]{1,0:T(1,128)S(1)}, s32[1,32]{1,0:T(1,128)}, u32[]{:S(2)}) copy-start(s32[1,32]{1,0:T(1,128)} %param.10) | copy-start | bytes 388
  63.4 88.9 %copy-start = (f32[2,128]{1,0:T(2,128)S(1)}, f32[2,128]{1,0:T(2,128)}, u32[]{:S(2)}) copy-start(f32[2,128]{1,0:T(2,128)} %param.13) | copy-start | bytes 3076
Sparse Core Ops, SparseCore 0:
  63.5 128.1 all-gather.2
where the time goes:
time: 230 us
  blocking collectives  97.2 us (42%)
  waiting for transfers between devices  58.3 us (25%)
  local copies, waits for them, and re-layouts  23.5 us (10%)
  starting transfers between devices  16.4 us (7%)
  between operations  14.2 us (6%)
  matrix products  12.9 us (6%)
  other arithmetic  7.15 us (3%)
    unnamed x1, blocking collectives  80 us
    all_gather x1, waiting for transfers between devices, local(): lax.all_gather(tokens, 'mp', axis=0, tiled=True)  39.4 us
    all_to_all x1, waiting for transfers between devices, local(): lax.all_to_all(send_rows, 'dp', split_axis=0, concat_axis=0, tiled=True)  18.9 us
    all_to_all x1, blocking collectives, local(): return lax.all_to_all(result, 'mp', split_axis=0, concat_axis=1, tiled=True)  17.2 us
    scatter x1, local copies, waits for them, and re-layouts, local(): jnp.zeros((n_groups, capacity, width), jnp.bfloat16).at[dest_group, rank]  10.3 us
    unnamed x1, matrix products  9.44 us
    all_to_all x1, starting transfers between devices, local(): lax.all_to_all(send_slots, 'dp', split_axis=0, concat_axis=0, tiled=True)  9.09 us
    unnamed x8, local copies, waits for them, and re-layouts  8.16 us
  transfers between devices with their start and end apart: 3, of which 2 were waited for; matrix products, arithmetic and copies ran while one was open for 10% of the time, Pallas kernels for 0%

commit v1 on v0

--- a/solution.py
+++ b/solution.py
@@ -4,6 +4,13 @@
 from jax.sharding import PartitionSpec as P
 
 HD = 128
+
+
+def exchange_gather(shard, axis, dim):
+    count = lax.axis_size(axis)
+    shards = jnp.stack([shard for _ in range(count)])
+    shards = lax.all_to_all(shards, axis, split_axis=0, concat_axis=0)
+    return jnp.concatenate(shards, axis=dim)
 
 
 def norm_rows(rows, gain):
@@ -42,7 +49,7 @@
     placing = (flat_slots[None, :] == positions[:, None].astype(jnp.float32)).astype(jnp.bfloat16)
     tokens = jnp.dot(placing, flat_rows, preferred_element_type=jnp.float32).astype(jnp.bfloat16)
     group_rows, group_ids = (
-        lax.all_gather(tokens, "mp", axis=0, tiled=True),
+        exchange_gather(tokens, "mp", 0),
         lax.all_gather(image_ids[0].astype(jnp.bfloat16), "mp", axis=0, tiled=True),
     )
     count = group_rows.shape[0]

time: 230 us -> 472 us (2.05)
  the two profiles are of different devices: /device:TPU:8 before, /device:TPU:24 now
where the time goes in v1:
time: 472 us; the launch traced here: 471 us
  blocking collectives  373 us (79%)
  local copies, waits for them, and re-layouts  29.7 us (6%)
  starting transfers between devices  27.8 us (6%)
  waiting for transfers between devices  20.5 us (4%)
  matrix products  12.1 us (3%)
  other arithmetic  7.15 us (2%)
    unnamed x1, blocking collectives  360 us
    all_to_all x1, waiting for transfers between devices, local(): lax.all_to_all(send_rows, 'dp', split_axis=0, concat_axis=0, tiled=True)  20.5 us
    all_to_all x1, blocking collectives, local(): return lax.all_to_all(result, 'mp', split_axis=0, concat_axis=1, tiled=True)  13.8 us
    all_to_all x1, starting transfers between devices, exchange_gather(): shards = lax.all_to_all(shards, axis, split_axis=0, concat_axis=0)  11.7 us
    scatter x1, local copies, waits for them, and re-layouts, local(): jnp.zeros((n_groups, capacity, width), jnp.bfloat16).at[dest_group, rank]  10.3 us
    unnamed x1, matrix products  9.45 us
  transfers between devices with their start and end apart: 3, of which 1 were waited for; matrix products, arithmetic and copies ran while one was open for 5% of the time, Pallas kernels for 0%

profile of v1, /device:TPU:24, one launch (start us, length us, event | category | flops | bytes accessed | tf_op | source)
XLA Modules:
  0.0 471.4 jit_solution(10508030553364314464)
XLA Ops:
  0.0 0.9 convert_reduce_fusion.1
  0.9 0.7 fusion.39
  1.6 0.7 convert_element_type.105
  2.2 2.1 scatter_fusion
  4.3 0.7 copy.22
  5.0 8.9 %all-to-all-start = ((bf16[16,1,4]{2,1,0:T(2,128)(2,1)}), bf16[16,1,4]{2,1,0:T(2,128)(2,1)S(1)}, u32[]{:S(2)}, u32[]{:S(2)}) async-start(bf16[16,1,4]{2,1,0:T(2,128)(2,1)} %copy.22), calls=%async_computation | async-start | bytes 16384 | tf_op jit(solution)/shard_map/all_to_all | solution.py:45
  13.9 1.2 convert_reduce_fusion
  15.1 1.3 fusion.7
  16.3 1.2 fusion.9
  17.5 1.2 broadcast_in_dim.11
  18.7 10.3 %scatter_fusion.1 = bf16[16,4,6144]{2,1,0:T(4,128)(2,1)} fusion(bf16[16,4,6144]{2,1,0:T(4,128)(2,1)} %broadcast_in_dim.11, s32[32]{0:T(128)S(1)} %fusion.39, bf16[32,6144]{1,0:T(8,128)(2,1)S(1)} %fusion.9), kind=kCustom, calls=%fused_computation.1 | custom fusion | bytes 1179904 | tf_op jit(solution)/shard_map/scatter | solution.py:36
  29.1 7.1 %all-to-all-start.1 = ((bf16[16,4,6144]{2,1,0:T(4,128)(2,1)}), bf16[16,4,6144]{2,1,0:T(4,128)(2,1)S(1)}, u32[]{:S(2)}, u32[]{:S(2)}) async-start(bf16[16,4,6144]{2,1,0:T(4,128)(2,1)} %scatter_fusion.1), calls=%async_computation.1 | async-start | bytes 1572864 | tf_op jit(solution)/shard_map/all_to_all | solution.py:44
  36.3 20.5 %all-to-all-done.1 = bf16[16,4,6144]{2,1,0:T(4,128)(2,1)S(1)} async-done(((bf16[16,4,6144]{2,1,0:T(4,128)(2,1)}), bf16[16,4,6144]{2,1,0:T(4,128)(2,1)S(1)}, u32[]{:S(2)}, u32[]{:S(2)}) %all-to-all-start.1) | async-done | bytes 786464 | tf_op jit(solution)/shard_map/all_to_all | solution.py:44
  57.3 6.0 %stack.2 = bf16[32,32,6144]{2,1,0:T(8,128)(2,1)} broadcast(bf16[32,6144]{1,0:T(8,128)(2,1)S(1)} %convolution_convert_fusion), dimensions={1,2} | broadcast | bytes 12976128 | tf_op jit(solution)/shard_map/stack | solution.py:11
  63.4 11.7 %all-to-all-start.2 = ((bf16[32,32,6144]{2,1,0:T(8,128)(2,1)}), bf16[32,32,6144]{2,1,0:T(8,128)(2,1)}, u32[]{:S(2)}, u32[]{:S(2)}) async-start(bf16[32,32,6144]{2,1,0:T(8,128)(2,1)} %stack.2), calls=%async_computation.2 | async-start | bytes 25165824 | tf_op jit(solution)/shard_map/all_to_all | solution.py:12
  75.2 6.7 %copy.23 = bf16[3,6144,128]{1,2,0:T(8,128)(2,1)} copy(bf16[3,6144,128]{2,1,0:T(8,128)(2,1)} %param.12) | data formatting | bytes 9437184 | tf_op args[5]
  81.8 1.3 dynamic-slice
  84.0 359.6 %all-reduce = bf16[1024]{0:T(1024)(128)(2,1)S(1)} all-reduce(bf16[1024]{0:T(1024)(128)(2,1)S(1)} %dynamic-update-slice), channel_id=2, replica_groups=mesh['dp'=16,'mp'=32] {'mp'}, use_global_device_ids=true, to_apply=%add | all-reduce | flops 1024 | bytes 4096
  443.6 9.5 %fusion.42 = f32[1024,384]{0,1:S(1)} fusion(bf16[1024,6144]{1,0:T(8,128)(2,1)} %bitcast.4, bf16[6144,384]{0,1:T(8,128)(2,1)} %bitcast.93), kind=kOutput, calls=%fused_computation.73 | convolution fusion | flops 4831838208 | bytes 18874368
  453.3 1.0 fusion.1
  454.3 1.0 fusion
  455.3 1.4 fusion.4
  456.9 13.8 %all_to_all.38 = bf16[32,32,128]{2,1,0:T(8,128)(2,1)S(1)} all-to-all(bf16[32,32,128]{2,1,0:T(8,128)(2,1)S(1)} %bitcast.98), channel_id=1, replica_groups=mesh['dp'=16,'mp'=32] {'mp'}, dimensions={0} | all-to-all | bytes 524288 | tf_op jit(solution)/shard_map/all_to_all | solution.py:74
  470.7 0.7 copy_bitcast_fusion
  (25 shorter events, 1.3 us)
Async XLA Ops:
  5.0 24.1 %all-to-all-start = ((bf16[16,1,4]{2,1,0:T(2,128)(2,1)}), bf16[16,1,4]{2,1,0:T(2,128)(2,1)S(1)}, u32[]{:S(2)}, u32[]{:S(2)}) async-start(bf16[16,1,4]{2,1,0:T(2,128)(2,1)} %copy.22), calls=%async_computation | async-start | bytes 16384 | tf_op jit(solution)/shard_map/all_to_all | solution.py:45
  29.1 27.8 %all-to-all-start.1 = ((bf16[16,4,6144]{2,1,0:T(4,128)(2,1)}), bf16[16,4,6144]{2,1,0:T(4,128)(2,1)S(1)}, u32[]{:S(2)}, u32[]{:S(2)}) async-start(bf16[16,4,6144]{2,1,0:T(4,128)(2,1)} %scatter_fusion.1), calls=%async_computation.1 | async-start | bytes 1572864 | tf_op jit(solution)/shard_map/all_to_all | solution.py:44
  63.4 380.2 %all-to-all-start.2 = ((bf16[32,32,6144]{2,1,0:T(8,128)(2,1)}), bf16[32,32,6144]{2,1,0:T(8,128)(2,1)}, u32[]{:S(2)}, u32[]{:S(2)}) async-start(bf16[32,32,6144]{2,1,0:T(8,128)(2,1)} %stack.2), calls=%async_computation.2 | async-start | bytes 25165824 | tf_op jit(solution)/shard_map/all_to_all | solution.py:12
  75.1 8.6 %copy-start.1 = (s32[1,32]{1,0:T(1,128)S(1)}, s32[1,32]{1,0:T(1,128)}, u32[]{:S(2)}) copy-start(s32[1,32]{1,0:T(1,128)} %param.10) | copy-start | bytes 388
  75.1 368.5 %copy-start = (f32[2,128]{1,0:T(2,128)S(1)}, f32[2,128]{1,0:T(2,128)}, u32[]{:S(2)}) copy-start(f32[2,128]{1,0:T(2,128)} %param.13) | copy-start | bytes 3076
